TPU v7x, 32 devices: a whole 2x2x4 slice. The times are simulated.
32 devices in a mesh: dp: 4 (over z), tile: 4 (over x, core), seq: 2 (over y).
Axes of the slice: x: 2, y: 2, z: 4, core: 2. Of those that a mesh axis runs over, the one named last changes fastest.
Arguments:
- features: bfloat16 [4, 8, 16, 32, 128], P('dp', None, 'tile'), may hold values from -6 to 6
- lengths: int32 [4], P('dp'), may hold values from 1 to 8, as said below
- weight: bfloat16 [3456, 5120], P(('dp', 'tile'), 'seq'), may hold values from -0.109375 to 0.109375
- bias: bfloat16 [5120], P('seq'), may hold values from -3 to 3
- cotangent: bfloat16 [4, 8, 16, 32, 5120], P('dp', 'seq', 'tile'), may hold values from -6 to 6
Outputs:
- pose_tokens: bfloat16 [4, 8, 16, 32, 5120], P('dp', 'seq', 'tile')
- grad_features: bfloat16 [4, 8, 16, 32, 128], P('dp', None, 'tile')
- grad_weight: float32 [3456, 5120], P(('dp', 'tile'), 'seq')
- grad_bias: float32 [5120], P('seq')
Inputs may be any that keep to these rules, and one draw needn't show every extreme that they name: `lengths`: exactly one clip has 8 live frames; every other clip has at most 4.
All inputs are finite; a program needn't handle non-finite values.
Results may differ from a plain program's by a relative error of at most 0.005.
Values may be sent and summed in bfloat16 or wider, within the bound.
A program may use at most 512 MiB of HBM per device.

v0:
```python
import jax
import jax.numpy as jnp
from jax import lax
from jax.sharding import PartitionSpec as P


def pick(pieces, index):
    result = pieces[0]
    for place in range(1, len(pieces)):
        result = jnp.where(index == place, pieces[place], result)
    return result


def swap(value, axis, distance):
    count = lax.axis_size(axis)
    return lax.ppermute(value, axis, [(i, i ^ distance) for i in range(count)])


def sum_over(value, axes):
    for axis in axes:
        distance = 1
        while distance < lax.axis_size(axis):
            value = value + swap(value, axis, distance)
            distance *= 2
    return value


def exchange(parts, axis):
    me = lax.axis_index(axis)
    count = lax.axis_size(axis)
    by_offset = [pick(parts, me)]
    for offset in range(1, count):
        by_offset.append(swap(pick(parts, me ^ offset), axis, offset))
    return [pick(by_offset, me ^ source) for source in range(count)]


def neighbours(low_row, high_row, axis):
    count = lax.axis_size(axis)
    forward = [(i, i + 1) for i in range(count - 1)]
    backward = [(i + 1, i) for i in range(count - 1)]
    return (lax.ppermute(high_row, axis, forward), lax.ppermute(low_row, axis, backward))


def silu_grad(values):
    sigma = jax.nn.sigmoid(values)
    return sigma * (1.0 + values * (1.0 - sigma))


def shards(features, lengths, weight, bias, cotangent):
    seq_count = lax.axis_size("seq")
    local_feat = features[0]
    frame_count, row_count, col_count, chan_count = local_feat.shape
    row_total = frame_count * row_count * col_count
    share = weight.shape[1]
    frame_share = frame_count // seq_count
    frame_mask = (jnp.arange(frame_count) < lengths[0]).astype(jnp.float32)[:, None, None, None]
    cot = cotangent[0]
    received = exchange([cot[..., j * share : (j + 1) * share] for j in range(seq_count)], "seq")
    grad_out = jnp.concatenate(received, axis=0) * frame_mask.astype(jnp.bfloat16)
    flat_grad = grad_out.reshape(row_total, share)
    inner_vals = local_feat.astype(jnp.float32)
    hidden = (jax.nn.silu(inner_vals) * frame_mask).astype(jnp.bfloat16)
    above, below = neighbours(hidden[:, :1], hidden[:, -1:], "tile")
    padded = jnp.pad(
        jnp.concatenate([above, hidden, below], axis=1), ((1, 1), (0, 0), (1, 1), (0, 0))
    )
    wide = jnp.concatenate([padded[:, :, e : e + col_count] for e in range(3)], axis=3)
    columns = jnp.concatenate(
        [wide[a : a + frame_count, b : b + row_count] for a in range(3) for b in range(3)], axis=3
    ).reshape(row_total, 27 * chan_count)
    weight_term = lax.dot_general(
        columns, flat_grad, (((0,), (0,)), ((), ())), preferred_element_type=jnp.float32
    ).astype(jnp.bfloat16)
    grad_weight = lax.psum_scatter(
        weight_term, ("dp", "tile"), scatter_dimension=0, tiled=True
    ).astype(jnp.float32)
    grad_bias = sum_over(jnp.sum(flat_grad, axis=0, dtype=jnp.float32), ("tile", "dp"))
    full_weight = lax.all_gather(weight, ("dp", "tile"), axis=0, tiled=True)
    output = jnp.dot(columns, full_weight, preferred_element_type=jnp.float32)
    tokens = (
        (output.reshape(frame_count, row_count, col_count, share) + bias.astype(jnp.float32))
        * frame_mask
    ).astype(jnp.bfloat16)
    pose_tokens = jnp.concatenate(
        exchange(
            [tokens[j * frame_share : (j + 1) * frame_share] for j in range(seq_count)], "seq"
        ),
        axis=3,
    )
    spread = lax.dot_general(
        flat_grad, full_weight, (((1,), (1,)), ((), ())), preferred_element_type=jnp.float32
    ).reshape(frame_count, row_count, col_count, 27 * chan_count)
    total = jnp.zeros((frame_count, row_count + 2, col_count, chan_count), jnp.float32)
    for a in range(3):
        for b in range(3):
            start = (a * 3 + b) * 3 * chan_count
            first = spread[..., start : start + chan_count]
            second = spread[..., start + chan_count : start + 2 * chan_count]
            third = spread[..., start + 2 * chan_count : start + 3 * chan_count]
            none = ((0, 0), (0, 0))
            joined = (
                jnp.pad(first[:, :, 1:], (*none, (0, 1), (0, 0)))
                + second
                + jnp.pad(third[:, :, :-1], (*none, (1, 0), (0, 0)))
            )
            kept = joined[max(0, 1 - a) : frame_count - max(0, a - 1)]
            total = total + jnp.pad(
                kept, ((max(0, a - 1), max(0, 1 - a)), (b, 2 - b), (0, 0), (0, 0))
            )
    from_above, from_below = neighbours(total[:, :1], total[:, -1:], "tile")
    rims = jnp.concatenate([from_above, jnp.zeros_like(total[:, 2:-2]), from_below], axis=1)
    grad_hidden = sum_over(total[:, 1:-1] + rims, ("seq",))
    grad_features = (silu_grad(inner_vals) * grad_hidden * frame_mask).astype(jnp.bfloat16)
    return (pose_tokens[None], grad_features[None], grad_weight, grad_bias)


def solution(mesh):
    return jax.shard_map(
        shards,
        mesh=mesh,
        in_specs=(
            P("dp", None, "tile", None, None),
            P("dp"),
            P(("dp", "tile"), "seq"),
            P("seq"),
            P("dp", "seq", "tile", None, None),
        ),
        out_specs=(
            P("dp", "seq", "tile", None, None),
            P("dp", None, "tile", None, None),
            P(("dp", "tile"), "seq"),
            P("seq"),
        ),
        check_vma=False,
    )
```

profile of v0, /device:TPU:0, one launch (start us, length us, event | category | flops | bytes accessed | tf_op | source)
XLA Modules:
  0.0 396.1 jit_solution(2411242803760982149)
XLA Ops:
  7.2 0.0 all-gather.2.cloned.1.call-start
  7.2 0.7 all-gather.2.cloned.1.call-update
  7.9 0.0 reduce-scatter.2.cloned.1.call-start
  8.0 2.8 broadcast_select_fusion.1
  10.8 3.0 collective-permute-start.3
  14.5 56.3 %collective-permute-done.3 = bf16[4,4,32,2560]{3,2,1,0:T(8,128)(2,1)} collective-permute-done((bf16[4,4,32,2560]{3,2,1,0:T(8,128)(2,1)S(1)}, bf16[4,4,32,2560]{3,2,1,0:T(8,128)(2,1)}, u32[]{:S(2)}, u32[]{:S(2)}) %collective-permute-start.3) | collective-permute-done | bytes 2621472 | tf_op jit(solution)/shard_map/ppermute | solution.py:16
  70.8 5.0 %broadcast_select_fusion.4 = (bf16[4,4,32,2560]{3,2,1,0:T(8,128)(2,1)S(1)}, bf16[4,4,32,2560]{3,2,1,0:T(8,128)(2,1)}) fusion(bf16[4,4,32,2560]{3,2,1,0:T(8,128)(2,1)} %collective-permute-done.3, pred[]{:T(512)S(6)} %eq.4, bf16[4,4,32,5120]{3,2,1,0:T(8,128)(2,1)} %bitcast.30, pred[]{:T(512)S(6)} %eq.5), kind=kLoop, calls=%fused_computation.13 | loop fusion | flops 3932160 | bytes 13107202 | tf_op jit(solution)/shard_map/jit(_where)/select_n | solution.py:10
  75.8 29.9 %all-gather.2.cloned.1.call-done = bf16[3456,2560]{1,0:T(8,128)(2,1)} async-done(((bf16[216,2560]{1,0:T(8,128)(2,1)}), bf16[3456,2560]{1,0:T(8,128)(2,1)}) %all-gather.2.cloned.1.call-update) | async-done | bytes 17694736 | tf_op jit(solution)/shard_map/all_gather | solution.py:78
  105.7 26.6 %fusion = f32[8,4,32,3456]{3,2,1,0:T(8,128)} fusion(bf16[3456,2560]{1,0:T(8,128)(2,1)} %all-gather.2.cloned.1.call-done, bf16[4,4,32,2560]{3,2,1,0:T(8,128)(2,1)} %get-tuple-element.32, bf16[4,4,32,2560]{3,2,1,0:T(8,128)(2,1)S(1)} %get-tuple-element.31, bf16[8]{0:T(256)(128)(2,1)S(1)} %fusion.26), kind=kOutput, calls=%fused_computation.1 | convolution fusion | flops 18124636160 | bytes 37093392 | tf_op jit(solution)/shard_map/dot_general | solution.py:90
  132.3 5.1 %fusion.27 = (f32[8,4,31,128]{3,2,1,0:T(8,128)S(1)}, f32[8,4,31,128]{3,2,1,0:T(8,128)S(1)}, f32[8,4,31,128]{3,2,1,0:T(8,128)S(1)}, f32[8,4,31,128]{3,2,1,0:T(8,1...) fusion(f32[8,4,32,3456]{3,2,1,0:T(8,128)} %fusion), kind=kLoop, calls=%fused_computation.75 | loop fusion | bytes 18284544 | tf_op jit(solution)/shard_map/slice | solution.py:102
  137.4 3.5 fusion.28
  140.8 0.4 pad_add_fusion.1
  141.2 0.4 pad_add_fusion.3
  141.6 0.0 copy-start.2
  141.6 0.4 pad_add_fusion.5
  141.9 0.5 pad_add_fusion
  142.5 1.3 collective-permute-start.5
  143.8 3.0 collective-permute-start.4
  146.8 0.1 pad.125.clone
  146.9 0.9 collective-permute-done.4
  147.8 0.1 slice_add_fusion
  147.9 1.6 collective-permute-start.6
  149.5 11.7 %collective-permute-done.6 = f32[8,4,32,128]{3,2,1,0:T(8,128)S(1)} collective-permute-done((f32[8,4,32,128]{3,2,1,0:T(8,128)S(1)}, f32[8,4,32,128]{3,2,1,0:T(8,128)S(1)}, u32[]{:S(2)}, u32[]{:S(2)}) %collective-permute-start.6) | collective-permute-done | bytes 524320 | tf_op jit(solution)/shard_map/ppermute | solution.py:16
  161.2 1.0 fusion.25
  162.3 1.3 collective-permute-start.1
  163.6 4.1 %collective-permute-start = (bf16[8,1,32,128]{3,2,1,0:T(8,128)(2,1)S(1)}, bf16[8,1,32,128]{3,2,1,0:T(8,128)(2,1)S(1)}, u32[]{:S(2)}, u32[]{:S(2)}) collective-permute-start(bf16[8,1,32,128]{3,2,1,0:T(8,128)(2,1)S(1)} %get-tuple-element.42), channel_id=1, source_target_pairs={{0,2},{2,4},{4,6},{1,3},{3,5},{5,7},{8,10},{10,12},{12,14},{9,11},... | collective-permute-start | bytes 196616 | tf_op jit(solution)/shard_map/ppermute | solution.py:41
  167.7 0.7 collective-permute-done
  168.4 0.2 select_maximum_fusion
  168.6 0.3 fusion.30
  168.9 0.2 pad_maximum_fusion
  169.2 0.1 slice_dynamic-update-slice_fusion.8
  169.3 0.1 slice_dynamic-update-slice_fusion.7
  169.4 0.0 copy-start
  169.4 0.1 slice_dynamic-update-slice_fusion.6
  169.6 0.1 slice_dynamic-update-slice_fusion.5
  169.7 0.1 slice_dynamic-update-slice_fusion.4
  169.9 0.1 slice_dynamic-update-slice_fusion.3
  170.0 0.1 slice_dynamic-update-slice_fusion.2
  170.2 0.1 slice_dynamic-update-slice_fusion.1
  170.4 0.1 slice_dynamic-update-slice_fusion
  170.5 2.9 copy-done.3
  173.4 21.5 %bitcast_convert_fusion = bf16[3456,2560]{1,0:T(8,128)(2,1)} fusion(bf16[8,4,32,3456]{3,2,1,0:T(8,128)(2,1)S(1)} %slice_dynamic-update-slice_fusion, bf16[4,4,32,2560]{3,2,1,0:T(8,128)(2,1)S(1)} %copy-done, bf16[4,4,32,2560]{3,2,1,0:T(8,128)(2,1)S(1)} %get-tuple-element.31, bf16[8]{0:T(256)(128)(2,1)S(1)} %fusion.26), kind=kOutput, calls=%fused_computation | convolution fusion | flops 18133483520 | bytes 30015504 | tf_op jit(solution)/shard_map/dot_general | solution.py:71
  194.9 0.0 reduce-scatter.2.cloned.1.call-update
  194.9 0.7 copy-done.4
  195.6 23.9 %multiply_convert_fusion = bf16[8,4,32,2560]{3,2,1,0:T(8,128)(2,1)S(1)} fusion(bf16[8,4,32,3456]{3,2,1,0:T(8,128)(2,1)} %copy-done.3, bf16[3456,2560]{1,0:T(8,128)(2,1)} %all-gather.2.cloned.1.call-done, f32[8]{0:T(128)S(1)} %copy-done.6, f32[2560]{0:T(1024)S(1)} %convert_element_type.90), kind=kOutput, calls=%fused_computation.6 | convolution fusion | flops 18127257600 | bytes 30025760 | tf_op jit(solution)/shard_map/dot_general | solution.py:79
  219.5 0.0 copy-start.1
  219.5 0.3 broadcast_select_fusion.3
  219.8 1.6 collective-permute-start.2
  221.4 0.3 copy-done.1
  221.7 1.5 convert_reduce_fusion
  223.3 2.2 collective-permute-start.7
  225.5 0.8 collective-permute-done.7
  226.3 2.6 collective-permute-start.8
  228.9 1.7 collective-permute-done.8
  230.6 1.5 collective-permute-start.9
  232.1 2.2 collective-permute-done.9
  234.3 2.4 collective-permute-start.10
  236.7 2.3 collective-permute-done.10
  239.0 0.6 add.205
  239.6 38.8 %collective-permute-done.2 = bf16[4,4,32,2560]{3,2,1,0:T(8,128)(2,1)S(1)} collective-permute-done((bf16[4,4,32,2560]{3,2,1,0:T(8,128)(2,1)S(1)}, bf16[4,4,32,2560]{3,2,1,0:T(8,128)(2,1)S(1)}, u32[]{:S(2)}, u32[]{:S(2)}) %collective-permute-start.2) | collective-permute-done | bytes 2621472 | tf_op jit(solution)/shard_map/ppermute | solution.py:16
  278.4 0.5 broadcast_select_fusion.6
  278.9 3.0 maximum_bitcast_fusion
  281.9 104.5 %reduce-scatter.2.cloned.1.call-done = bf16[216,2560]{1,0:T(8,128)(2,1)} async-done(((bf16[3456,2560]{1,0:T(8,128)(2,1)}), bf16[216,2560]{1,0:T(8,128)(2,1)}) %reduce-scatter.2.cloned.1.call-update) | async-done | bytes 1105936 | tf_op jit(solution)/shard_map/reduce_scatter | solution.py:74
  386.4 2.9 convert_element_type.95
  (19 shorter events, 0.1 us)
Async XLA Ops:
  7.2 98.6 %all-gather.2.cloned.1.call-start = ((), (), s32[]{:S(2)}) async-start(), calls=%async_computation.1 | async-start | bytes 18800640 | tf_op jit(solution)/shard_map/all_gather | solution.py:78
  7.9 378.5 %reduce-scatter.2.cloned.1.call-start = ((), (), s32[]{:S(2)}) async-start(), calls=%async_computation.2 | async-start | bytes 18800640 | tf_op jit(solution)/shard_map/reduce_scatter | solution.py:74
  10.8 60.0 %collective-permute-start.3 = (bf16[4,4,32,2560]{3,2,1,0:T(8,128)(2,1)S(1)}, bf16[4,4,32,2560]{3,2,1,0:T(8,128)(2,1)}, u32[]{:S(2)}, u32[]{:S(2)}) collective-permute-start(bf16[4,4,32,2560]{3,2,1,0:T(8,128)(2,1)S(1)} %broadcast_select_fusion.1), channel_id=1, source_target_pairs={{0,1},{1,0},{2,3},{3,2},{4,5},{5,4},{6,7},{7,6},{8,9},{9,8},{10,11... | collective-permute-start | bytes 7864328 | tf_op jit(solution)/shard_map/ppermute | solution.py:16
  141.6 19.7 %copy-start.2 = (bf16[1,8,4,32,128]{4,3,2,1,0:T(8,128)(2,1)S(1)}, bf16[1,8,4,32,128]{4,3,2,1,0:T(8,128)(2,1)}, u32[]{:S(2)}) copy-start(bf16[1,8,4,32,128]{4,3,2,1,0:T(8,128)(2,1)} %param.5) | copy-start | bytes 786436
  142.5 4.4 %collective-permute-start.5 = (f32[8,1,32,128]{3,2,1,0:T(8,128)S(1)}, f32[8,1,32,128]{3,2,1,0:T(8,128)S(1)}, u32[]{:S(2)}, u32[]{:S(2)}) collective-permute-start(f32[8,1,32,128]{3,2,1,0:T(8,128)S(1)} %get-tuple-element.36), channel_id=1, source_target_pairs={{2,0},{4,2},{6,4},{3,1},{5,3},{7,5},{10,8},{12,10},{14,12},{11,9},... | collective-permute-start | bytes 393224 | tf_op jit(solution)/shard_map/ppermute | solution.py:41
  143.8 4.0 %collective-permute-start.4 = (f32[8,1,32,128]{3,2,1,0:T(8,128)S(1)}, f32[8,1,32,128]{3,2,1,0:T(8,128)S(1)}, u32[]{:S(2)}, u32[]{:S(2)}) collective-permute-start(f32[8,1,32,128]{3,2,1,0:T(8,128)S(1)} %get-tuple-element.35), channel_id=1, source_target_pairs={{0,2},{2,4},{4,6},{1,3},{3,5},{5,7},{8,10},{10,12},{12,14},{9,11},... | collective-permute-start | bytes 393224 | tf_op jit(solution)/shard_map/ppermute | solution.py:41
  147.9 13.3 %collective-permute-start.6 = (f32[8,4,32,128]{3,2,1,0:T(8,128)S(1)}, f32[8,4,32,128]{3,2,1,0:T(8,128)S(1)}, u32[]{:S(2)}, u32[]{:S(2)}) collective-permute-start(f32[8,4,32,128]{3,2,1,0:T(8,128)S(1)} %slice_add_fusion), channel_id=1, source_target_pairs={{0,1},{1,0},{2,3},{3,2},{4,5},{5,4},{6,7},{7,6},{8,9},{9,8},{10,11... | collective-permute-start | bytes 1572872 | tf_op jit(solution)/shard_map/ppermute | solution.py:16
  149.5 19.7 %copy-start.5 = (f32[8]{0:T(128)}, f32[8]{0:T(128)S(1)}, u32[]{:S(2)}) copy-start(f32[8]{0:T(128)S(1)} %compare_convert_fusion) | copy-start | bytes 100
  162.3 5.4 %collective-permute-start.1 = (bf16[8,1,32,128]{3,2,1,0:T(8,128)(2,1)S(1)}, bf16[8,1,32,128]{3,2,1,0:T(8,128)(2,1)S(1)}, u32[]{:S(2)}, u32[]{:S(2)}) collective-permute-start(bf16[8,1,32,128]{3,2,1,0:T(8,128)(2,1)S(1)} %get-tuple-element.43), channel_id=1, source_target_pairs={{2,0},{4,2},{6,4},{3,1},{5,3},{7,5},{10,8},{12,10},{14,12},{11,9},... | collective-permute-start | bytes 196616 | tf_op jit(solution)/shard_map/ppermute | solution.py:41
  163.6 4.8 %collective-permute-start = (bf16[8,1,32,128]{3,2,1,0:T(8,128)(2,1)S(1)}, bf16[8,1,32,128]{3,2,1,0:T(8,128)(2,1)S(1)}, u32[]{:S(2)}, u32[]{:S(2)}) collective-permute-start(bf16[8,1,32,128]{3,2,1,0:T(8,128)(2,1)S(1)} %get-tuple-element.42), channel_id=1, source_target_pairs={{0,2},{2,4},{4,6},{1,3},{3,5},{5,7},{8,10},{10,12},{12,14},{9,11},... | collective-permute-start | bytes 196616 | tf_op jit(solution)/shard_map/ppermute | solution.py:41
  169.4 4.0 %copy-start = (bf16[4,4,32,2560]{3,2,1,0:T(8,128)(2,1)S(1)}, bf16[4,4,32,2560]{3,2,1,0:T(8,128)(2,1)}, u32[]{:S(2)}) copy-start(bf16[4,4,32,2560]{3,2,1,0:T(8,128)(2,1)} %get-tuple-element.32) | copy-start | bytes 7864324
  170.5 2.9 copy-start.3
  194.9 0.7 copy-start.4
  194.9 0.7 copy-start.6
  219.5 2.2 copy-start.1
  219.8 58.6 %collective-permute-start.2 = (bf16[4,4,32,2560]{3,2,1,0:T(8,128)(2,1)S(1)}, bf16[4,4,32,2560]{3,2,1,0:T(8,128)(2,1)S(1)}, u32[]{:S(2)}, u32[]{:S(2)}) collective-permute-start(bf16[4,4,32,2560]{3,2,1,0:T(8,128)(2,1)S(1)} %broadcast_select_fusion.3), channel_id=1, source_target_pairs={{0,1},{1,0},{2,3},{3,2},{4,5},{5,4},{6,7},{7,6},{8,9},{9,8},{10,11... | collective-permute-start | bytes 7864328 | tf_op jit(solution)/shard_map/ppermute | solution.py:16
  223.3 3.1 collective-permute-start.7
  226.3 4.2 %collective-permute-start.8 = (f32[2560]{0:T(1024)S(1)}, f32[2560]{0:T(1024)S(1)}, u32[]{:S(2)}, u32[]{:S(2)}) collective-permute-start(f32[2560]{0:T(1024)S(1)} %add.202), channel_id=1, source_target_pairs={{0,4},{2,6},{4,0},{6,2},{1,5},{3,7},{5,1},{7,3},{8,12},{10,14},{12... | collective-permute-start | bytes 30728 | tf_op jit(solution)/shard_map/ppermute | solution.py:16
  230.6 3.7 collective-permute-start.9
  234.3 4.7 %collective-permute-start.10 = (f32[2560]{0:T(1024)S(1)}, f32[2560]{0:T(1024)S(1)}, u32[]{:S(2)}, u32[]{:S(2)}) collective-permute-start(f32[2560]{0:T(1024)S(1)} %add.204), channel_id=1, source_target_pairs={{0,16},{8,24},{16,0},{24,8},{1,17},{9,25},{17,1},{25,9},{2,18},{10... | collective-permute-start | bytes 30728 | tf_op jit(solution)/shard_map/ppermute | solution.py:16
Sparse Core Ops, SparseCore 0:
  9.6 96.0 all-gather.1
  195.1 191.3 reduce-scatter.1
where the time goes:
time: 396 us
  waiting for transfers between devices  251 us (63%)
  matrix products  72 us (18%)
  starting transfers between devices  24.7 us (6%)
  other arithmetic  23.3 us (6%)
  between operations  15 us (4%)
  local copies, waits for them, and re-layouts  10.7 us (3%)
    ppermute x7, waiting for transfers between devices, swap(): return lax.ppermute(value, axis, [(i, i ^ distance) for i in range(count)])  114 us
    reduce_scatter x1, waiting for transfers between devices, shards(): lax.psum_scatter(weight_term, ('dp', 'tile'), scatter_dimension=0, tiled=...  104 us
    all_gather x1, waiting for transfers between devices, shards(): full_weight = lax.all_gather(weight, ('dp', 'tile'), axis=0, tiled=True)  29.9 us
    dot_general x1, matrix products, shards(): lax.dot_general(flat_grad, full_weight, (((1,), (1,)), ((), ())), preferr...  26.6 us
    dot_general x1, matrix products, shards(): output = jnp.dot(columns, full_weight, preferred_element_type=jnp.float32)  23.9 us
    dot_general x1, matrix products, shards(): lax.dot_general(columns, flat_grad, (((0,), (0,)), ((), ())), preferred_e...  21.5 us
    ppermute x7, starting transfers between devices, swap(): return lax.ppermute(value, axis, [(i, i ^ distance) for i in range(count)])  14.9 us
    select_n x4, other arithmetic, pick(): result = jnp.where(index == place, pieces[place], result)  8.58 us
  transfers between devices with their start and end apart: 13, of which 11 were waited for; matrix products, arithmetic and copies ran while one was open for 10% of the time, Pallas kernels for 0%

commit v1 on v0

--- a/solution.py
+++ b/solution.py
@@ -75,7 +75,23 @@
         weight_term, ("dp", "tile"), scatter_dimension=0, tiled=True
     ).astype(jnp.float32)
     grad_bias = sum_over(jnp.sum(flat_grad, axis=0, dtype=jnp.float32), ("tile", "dp"))
-    full_weight = lax.all_gather(weight, ("dp", "tile"), axis=0, tiled=True)
+    cores_n = lax.axis_size(("dp", "tile"))
+    sheets = []
+    for idx in [*range(cores_n)]:
+        sheets.append((idx, (idx + 1) % cores_n))
+    by_rank = []
+    for idx in tuple(range(cores_n)):
+        by_rank.append((idx, (idx - 1) % cores_n))
+    taken_in, far_arr = ([weight], [weight])
+    for _ in range(cores_n // 2):
+        taken_in.append(lax.ppermute(taken_in[-1], ("dp", "tile"), sheets))
+    for _ in [*range((cores_n - 1) // 2)]:
+        far_arr.append(lax.ppermute(far_arr[-1], ("dp", "tile"), perm=by_rank))
+    full_weight = jnp.roll(
+        jnp.concatenate([*taken_in[::-1], *far_arr[1:]], axis=0),
+        (lax.axis_index(("dp", "tile")) - cores_n // 2) * weight.shape[0],
+        axis=0,
+    )
     output = jnp.dot(columns, full_weight, preferred_element_type=jnp.float32)
     tokens = (
         (output.reshape(frame_count, row_count, col_count, share) + bias.astype(jnp.float32))

time: 396 us -> 555 us (1.40)
  starting transfers between devices: 24.7 us -> 155 us
  local copies, waits for them, and re-layouts: 10.7 us -> 67.3 us
  waiting for transfers between devices: 251 us -> 218 us
    ppermute x0 -> x15, starting transfers between devices: none -> 114 us  [the longest x8 109 us: shards(): taken_in.append(lax.ppermute(taken_in[-1], ('dp', 'tile'), sheets))]
    ppermute x7, waiting for transfers between devices: 114 us -> 58.4 us  [swap(): return lax.ppermute(value, axis, [(i, i ^ distance) for i in range(count)])]
    unnamed x22 -> x89, local copies, waits for them, and re-layouts: 5.02 us -> 59.7 us
    ppermute x0 -> x15, waiting for transfers between devices: none -> 51.6 us  [the longest x8 51.6 us: shards(): taken_in.append(lax.ppermute(taken_in[-1], ('dp', 'tile'), sheets))]
    all_gather x1 -> x0, waiting for transfers between devices: 29.9 us -> none  [shards(): full_weight = lax.all_gather(weight, ('dp', 'tile'), axis=0, tiled=True)]
    ppermute x2, starting transfers between devices: 7.15 us -> 27.9 us  [neighbours(): lax.ppermute(high_row, axis, forward)]
  transfers between devices with their start and end apart: 13 -> 27, of which waited for: 11 -> 15; matrix products, arithmetic and copies ran while one was open for 10% -> 11% of each run, Pallas kernels for 0% -> 0%
where the time goes in v1:
time: 555 us; the launch traced here: 554 us
  waiting for transfers between devices  218 us (39%)
  starting transfers between devices  155 us (28%)
  matrix products  74.5 us (13%)
  local copies, waits for them, and re-layouts  67.3 us (12%)
  other arithmetic  23.3 us (4%)
  between operations  15 us (3%)
    ppermute x8, starting transfers between devices, shards(): taken_in.append(lax.ppermute(taken_in[-1], ('dp', 'tile'), sheets))  109 us
    reduce_scatter x1, waiting for transfers between devices, shards(): lax.psum_scatter(weight_term, ('dp', 'tile'), scatter_dimension=0, tiled=...  103 us
    unnamed x89, local copies, waits for them, and re-layouts  59.7 us
    ppermute x7, waiting for transfers between devices, swap(): return lax.ppermute(value, axis, [(i, i ^ distance) for i in range(count)])  58.4 us
    ppermute x8, waiting for transfers between devices, shards(): taken_in.append(lax.ppermute(taken_in[-1], ('dp', 'tile'), sheets))  51.6 us
    ppermute x2, starting transfers between devices, neighbours(): lax.ppermute(high_row, axis, forward)  27.9 us
    dot_general x1, matrix products, shards(): lax.dot_general(flat_grad, full_weight, (((1,), (1,)), ((), ())), preferr...  25.8 us
    dot_general x1, matrix products, shards(): lax.dot_general(columns, flat_grad, (((0,), (0,)), ((), ())), preferred_e...  24.6 us
  transfers between devices with their start and end apart: 27, of which 15 were waited for; matrix products, arithmetic and copies ran while one was open for 11% of the time, Pallas kernels for 0%

profile of v1, /device:TPU:0, one launch (start us, length us, event | category | flops | bytes accessed | tf_op | source)
XLA Modules:
  0.0 553.8 jit_solution(15807133512378389880)
XLA Ops:
  7.7 18.3 %collective-permute-done.2 = bf16[216,2560]{1,0:T(8,128)(2,1)S(1)} collective-permute-done((bf16[216,2560]{1,0:T(8,128)(2,1)}, bf16[216,2560]{1,0:T(8,128)(2,1)S(1)}, u32[]{:S(2)}, u32[]{:S(2)}) %collective-permute-start.2) | collective-permute-done | bytes 1105952 | tf_op jit(solution)/shard_map/ppermute | solution.py:87
  27.0 4.4 collective-permute-start.10
  31.5 13.2 %collective-permute-done.3 = bf16[216,2560]{1,0:T(8,128)(2,1)S(1)} collective-permute-done((bf16[216,2560]{1,0:T(8,128)(2,1)S(1)}, bf16[216,2560]{1,0:T(8,128)(2,1)S(1)}, u32[]{:S(2)}, u32[]{:S(2)}) %collective-permute-start.3) | collective-permute-done | bytes 1105952 | tf_op jit(solution)/shard_map/ppermute | solution.py:87
  44.7 5.9 %collective-permute-start.4 = (bf16[216,2560]{1,0:T(8,128)(2,1)S(1)}, bf16[216,2560]{1,0:T(8,128)(2,1)S(1)}, u32[]{:S(2)}, u32[]{:S(2)}) collective-permute-start(bf16[216,2560]{1,0:T(8,128)(2,1)S(1)} %collective-permute-done.3), channel_id=1, source_target_pairs={{0,2},{2,4},{4,6},{6,8},{8,10},{10,12},{12,14},{14,16},{16,18},{18... | collective-permute-start | bytes 3317768 | tf_op jit(solution)/shard_map/ppermute | solution.py:87
  50.7 11.6 %collective-permute-done.4 = bf16[216,2560]{1,0:T(8,128)(2,1)S(1)} collective-permute-done((bf16[216,2560]{1,0:T(8,128)(2,1)S(1)}, bf16[216,2560]{1,0:T(8,128)(2,1)S(1)}, u32[]{:S(2)}, u32[]{:S(2)}) %collective-permute-start.4) | collective-permute-done | bytes 1105952 | tf_op jit(solution)/shard_map/ppermute | solution.py:87
  62.3 14.3 %collective-permute-start.5 = (bf16[216,2560]{1,0:T(8,128)(2,1)S(1)}, bf16[216,2560]{1,0:T(8,128)(2,1)}, u32[]{:S(2)}, u32[]{:S(2)}) collective-permute-start(bf16[216,2560]{1,0:T(8,128)(2,1)S(1)} %collective-permute-done.4), channel_id=1, source_target_pairs={{0,2},{2,4},{4,6},{6,8},{8,10},{10,12},{12,14},{14,16},{16,18},{18... | collective-permute-start | bytes 3317768 | tf_op jit(solution)/shard_map/ppermute | solution.py:87
  76.6 4.7 collective-permute-done.5
  81.2 21.3 %collective-permute-start.6 = (bf16[216,2560]{1,0:T(8,128)(2,1)}, bf16[216,2560]{1,0:T(8,128)(2,1)S(1)}, u32[]{:S(2)}, u32[]{:S(2)}) collective-permute-start(bf16[216,2560]{1,0:T(8,128)(2,1)} %collective-permute-done.5), channel_id=1, source_target_pairs={{0,2},{2,4},{4,6},{6,8},{8,10},{10,12},{12,14},{14,16},{16,18},{18... | collective-permute-start | bytes 3317768 | tf_op jit(solution)/shard_map/ppermute | solution.py:87
  102.5 4.3 broadcast_select_fusion.1
  106.8 1.5 collective-permute-start.18
  109.4 20.2 %collective-permute-start.7 = (bf16[216,2560]{1,0:T(8,128)(2,1)S(1)}, bf16[216,2560]{1,0:T(8,128)(2,1)S(1)}, u32[]{:S(2)}, u32[]{:S(2)}) collective-permute-start(bf16[216,2560]{1,0:T(8,128)(2,1)S(1)} %collective-permute-done.6), channel_id=1, source_target_pairs={{0,2},{2,4},{4,6},{6,8},{8,10},{10,12},{12,14},{14,16},{16,18},{18... | collective-permute-start | bytes 3317768 | tf_op jit(solution)/shard_map/ppermute | solution.py:87
  130.6 1.4 collective-permute-done.7
  132.0 24.2 %collective-permute-start.8 = (bf16[216,2560]{1,0:T(8,128)(2,1)S(1)}, bf16[216,2560]{1,0:T(8,128)(2,1)}, u32[]{:S(2)}, u32[]{:S(2)}) collective-permute-start(bf16[216,2560]{1,0:T(8,128)(2,1)S(1)} %collective-permute-done.7), channel_id=1, source_target_pairs={{0,2},{2,4},{4,6},{6,8},{8,10},{10,12},{12,14},{14,16},{16,18},{18... | collective-permute-start | bytes 3317768 | tf_op jit(solution)/shard_map/ppermute | solution.py:87
  156.2 2.5 collective-permute-done.8
  158.7 22.6 %collective-permute-start.9 = (bf16[216,2560]{1,0:T(8,128)(2,1)}, bf16[216,2560]{1,0:T(8,128)(2,1)}, u32[]{:S(2)}, u32[]{:S(2)}) collective-permute-start(bf16[216,2560]{1,0:T(8,128)(2,1)} %collective-permute-done.8), channel_id=1, source_target_pairs={{0,2},{2,4},{4,6},{6,8},{8,10},{10,12},{12,14},{14,16},{16,18},{18... | collective-permute-start | bytes 3317768 | tf_op jit(solution)/shard_map/ppermute | solution.py:87
  182.0 3.7 broadcast_select_fusion.4
  185.8 3.4 constant_dynamic-update-slice_fusion.31
  189.2 2.4 constant_dynamic-update-slice_fusion.30
  193.8 2.4 constant_dynamic-update-slice_fusion.27
  196.2 1.1 constant_dynamic-update-slice_fusion.26
  197.3 1.1 constant_dynamic-update-slice_fusion.25
  198.4 1.1 constant_dynamic-update-slice_fusion.24
  199.6 1.1 constant_dynamic-update-slice_fusion.23
  201.7 1.1 constant_dynamic-update-slice_fusion.21
  203.9 1.1 constant_dynamic-update-slice_fusion.19
  205.0 2.4 constant_dynamic-update-slice_fusion.18
  207.4 2.3 constant_dynamic-update-slice_fusion.17
  210.8 2.3 constant_dynamic-update-slice_fusion.15
  213.1 2.3 constant_dynamic-update-slice_fusion.14
  216.5 1.1 constant_dynamic-update-slice_fusion.12
  217.5 2.3 constant_dynamic-update-slice_fusion.11
  219.9 1.1 constant_dynamic-update-slice_fusion.10
  221.0 1.1 constant_dynamic-update-slice_fusion.9
  224.2 1.1 constant_dynamic-update-slice_fusion.6
  225.3 1.1 constant_dynamic-update-slice_fusion.5
  227.5 1.1 constant_dynamic-update-slice_fusion.3
  228.6 2.3 constant_dynamic-update-slice_fusion.2
  231.0 2.3 constant_dynamic-update-slice_fusion.1
  234.3 25.8 %fusion = f32[8,4,32,3456]{3,2,1,0:T(8,128)} fusion(bf16[6912,2560]{1,0:T(8,128)(2,1)} %constant_dynamic-update-slice_fusion, s32[]{:T(128)S(6)} %select_n.54, bf16[4,4,32,2560]{3,2,1,0:T(8,128)(2,1)S(1)} %get-tuple-element.32, bf16[4,4,32,2560]{3,2,1,0:T(8,128)(2,1)S(1)} %get-tuple-element.31, bf16[8]{0:T(256)(128)(2,1)S(1)} %fusion.30), kind=kOutput, calls=%fused_computation.1 | convolution fusion | flops 18124636160 | bytes 37093396 | tf_op jit(solution)/shard_map/dot_general | solution.py:106
  260.1 5.0 fusion.31
  265.1 3.3 fusion.32
  270.1 23.5 %collective-permute-start.19 = (f32[8,1,32,128]{3,2,1,0:T(8,128)S(1)}, f32[8,1,32,128]{3,2,1,0:T(8,128)S(1)}, u32[]{:S(2)}, u32[]{:S(2)}) collective-permute-start(f32[8,1,32,128]{3,2,1,0:T(8,128)S(1)} %get-tuple-element.35), channel_id=1, source_target_pairs={{0,2},{2,4},{4,6},{1,3},{3,5},{5,7},{8,10},{10,12},{12,14},{9,11},... | collective-permute-start | bytes 393224 | tf_op jit(solution)/shard_map/ppermute | solution.py:41
  293.7 1.3 collective-permute-start.20
  295.1 3.8 collective-permute-done.20
  299.0 1.6 collective-permute-start.21
  300.6 10.6 %collective-permute-done.21 = f32[8,4,32,128]{3,2,1,0:T(8,128)S(1)} collective-permute-done((f32[8,4,32,128]{3,2,1,0:T(8,128)S(1)}, f32[8,4,32,128]{3,2,1,0:T(8,128)S(1)}, u32[]{:S(2)}, u32[]{:S(2)}) %collective-permute-start.21) | collective-permute-done | bytes 524320 | tf_op jit(solution)/shard_map/ppermute | solution.py:16
  312.3 4.4 collective-permute-start
  316.7 1.5 collective-permute-start.1
  318.2 1.6 collective-permute-done.1
  325.7 1.1 slice_dynamic-update-slice_fusion.3
  329.8 24.6 %bitcast_convert_fusion = bf16[3456,2560]{1,0:T(8,128)(2,1)} fusion(bf16[8,4,32,3456]{3,2,1,0:T(8,128)(2,1)} %slice_dynamic-update-slice_fusion, bf16[4,4,32,2560]{3,2,1,0:T(8,128)(2,1)S(1)} %get-tuple-element.32, bf16[4,4,32,2560]{3,2,1,0:T(8,128)(2,1)S(1)} %get-tuple-element.31, bf16[8]{0:T(256)(128)(2,1)S(1)} %fusion.30), kind=kOutput, calls=%fused_computation | convolution fusion | flops 18133483520 | bytes 30015504 | tf_op jit(solution)/shard_map/dot_general | solution.py:71
  355.1 24.1 %multiply_convert_fusion = bf16[8,4,32,2560]{3,2,1,0:T(8,128)(2,1)S(1)} fusion(bf16[8,4,32,3456]{3,2,1,0:T(8,128)(2,1)} %slice_dynamic-update-slice_fusion, bf16[6912,2560]{1,0:T(8,128)(2,1)} %constant_dynamic-update-slice_fusion, s32[]{:T(128)S(6)} %select_n.54, f32[8]{0:T(128)S(1)} %copy-done.24, f32[2560]{0:T(1024)S(1)} %convert_element_type.90), kind=kOutput, calls=%fused_computation.8 | convolution fusion | flops 18127257600 | bytes 30025764 | tf_op jit(solution)/shard_map/dot_general | solution.py:95
  379.5 1.6 collective-permute-start.17
  381.4 1.5 convert_reduce_fusion
  383.0 2.5 collective-permute-start.22
  386.6 3.4 collective-permute-done.23
  390.0 1.3 collective-permute-start.24
  391.3 2.4 collective-permute-done.24
  393.7 2.3 collective-permute-start.25
  396.1 3.6 collective-permute-done.25
  400.3 37.5 %collective-permute-done.17 = bf16[4,4,32,2560]{3,2,1,0:T(8,128)(2,1)S(1)} collective-permute-done((bf16[4,4,32,2560]{3,2,1,0:T(8,128)(2,1)S(1)}, bf16[4,4,32,2560]{3,2,1,0:T(8,128)(2,1)S(1)}, u32[]{:S(2)}, u32[]{:S(2)}) %collective-permute-start.17) | collective-permute-done | bytes 2621472 | tf_op jit(solution)/shard_map/ppermute | solution.py:16
  438.3 3.0 maximum_bitcast_fusion
  441.3 102.8 %reduce-scatter.2.cloned.1.call-done = bf16[216,2560]{1,0:T(8,128)(2,1)} async-done(((bf16[3456,2560]{1,0:T(8,128)(2,1)}), bf16[216,2560]{1,0:T(8,128)(2,1)}) %reduce-scatter.2.cloned.1.call-update) | async-done | bytes 1105936 | tf_op jit(solution)/shard_map/reduce_scatter | solution.py:74
  544.1 2.9 convert_element_type.95
  (114 shorter events, 29.8 us)
Async XLA Ops:
  7.2 537.0 %reduce-scatter.2.cloned.1.call-start = ((), (), s32[]{:S(2)}) async-start(), calls=%async_computation.1 | async-start | bytes 18800640 | tf_op jit(solution)/shard_map/reduce_scatter | solution.py:74
  7.2 18.8 %collective-permute-start.2 = (bf16[216,2560]{1,0:T(8,128)(2,1)}, bf16[216,2560]{1,0:T(8,128)(2,1)S(1)}, u32[]{:S(2)}, u32[]{:S(2)}) collective-permute-start(bf16[216,2560]{1,0:T(8,128)(2,1)} %param.7), channel_id=1, source_target_pairs={{0,2},{2,4},{4,6},{6,8},{8,10},{10,12},{12,14},{14,16},{16,18},{18... | collective-permute-start | bytes 3317768 | tf_op jit(solution)/shard_map/ppermute | solution.py:87
  26.0 1.0 copy-start.3
  27.0 17.6 %collective-permute-start.3 = (bf16[216,2560]{1,0:T(8,128)(2,1)S(1)}, bf16[216,2560]{1,0:T(8,128)(2,1)S(1)}, u32[]{:S(2)}, u32[]{:S(2)}) collective-permute-start(bf16[216,2560]{1,0:T(8,128)(2,1)S(1)} %collective-permute-done.2), channel_id=1, source_target_pairs={{0,2},{2,4},{4,6},{6,8},{8,10},{10,12},{12,14},{14,16},{16,18},{18... | collective-permute-start | bytes 3317768 | tf_op jit(solution)/shard_map/ppermute | solution.py:87
  27.0 23.6 %collective-permute-start.10 = (bf16[216,2560]{1,0:T(8,128)(2,1)}, bf16[216,2560]{1,0:T(8,128)(2,1)S(1)}, u32[]{:S(2)}, u32[]{:S(2)}) collective-permute-start(bf16[216,2560]{1,0:T(8,128)(2,1)} %param.7), channel_id=1, source_target_pairs={{0,30},{2,0},{4,2},{6,4},{8,6},{10,8},{12,10},{14,12},{16,14},{18,... | collective-permute-start | bytes 3317768 | tf_op jit(solution)/shard_map/ppermute | solution.py:89
  44.7 5.9 %copy-start.7 = (bf16[216,2560]{1,0:T(8,128)(2,1)}, bf16[216,2560]{1,0:T(8,128)(2,1)S(1)}, u32[]{:S(2)}) copy-start(bf16[216,2560]{1,0:T(8,128)(2,1)S(1)} %collective-permute-done.3) | copy-start | bytes 3317764
  44.7 17.6 %collective-permute-start.4 = (bf16[216,2560]{1,0:T(8,128)(2,1)S(1)}, bf16[216,2560]{1,0:T(8,128)(2,1)S(1)}, u32[]{:S(2)}, u32[]{:S(2)}) collective-permute-start(bf16[216,2560]{1,0:T(8,128)(2,1)S(1)} %collective-permute-done.3), channel_id=1, source_target_pairs={{0,2},{2,4},{4,6},{6,8},{8,10},{10,12},{12,14},{14,16},{16,18},{18... | collective-permute-start | bytes 3317768 | tf_op jit(solution)/shard_map/ppermute | solution.py:87
  50.6 131.4 %copy-start.5 = (bf16[216,2560]{1,0:T(8,128)(2,1)}, bf16[216,2560]{1,0:T(8,128)(2,1)S(1)}, u32[]{:S(2)}) copy-start(bf16[216,2560]{1,0:T(8,128)(2,1)S(1)} %collective-permute-done.10) | copy-start | bytes 3317764
  50.6 26.0 %collective-permute-start.11 = (bf16[216,2560]{1,0:T(8,128)(2,1)S(1)}, bf16[216,2560]{1,0:T(8,128)(2,1)S(1)}, u32[]{:S(2)}, u32[]{:S(2)}) collective-permute-start(bf16[216,2560]{1,0:T(8,128)(2,1)S(1)} %collective-permute-done.10), channel_id=1, source_target_pairs={{0,30},{2,0},{4,2},{6,4},{8,6},{10,8},{12,10},{14,12},{16,14},{18,... | collective-permute-start | bytes 3317768 | tf_op jit(solution)/shard_map/ppermute | solution.py:89
  62.3 119.7 %copy-start.11 = (bf16[216,2560]{1,0:T(8,128)(2,1)}, bf16[216,2560]{1,0:T(8,128)(2,1)S(1)}, u32[]{:S(2)}) copy-start(bf16[216,2560]{1,0:T(8,128)(2,1)S(1)} %collective-permute-done.4) | copy-start | bytes 3317764
  62.3 18.9 %collective-permute-start.5 = (bf16[216,2560]{1,0:T(8,128)(2,1)S(1)}, bf16[216,2560]{1,0:T(8,128)(2,1)}, u32[]{:S(2)}, u32[]{:S(2)}) collective-permute-start(bf16[216,2560]{1,0:T(8,128)(2,1)S(1)} %collective-permute-done.4), channel_id=1, source_target_pairs={{0,2},{2,4},{4,6},{6,8},{8,10},{10,12},{12,14},{14,16},{16,18},{18... | collective-permute-start | bytes 3317768 | tf_op jit(solution)/shard_map/ppermute | solution.py:87
  76.6 105.4 %copy-start.9 = (bf16[216,2560]{1,0:T(8,128)(2,1)}, bf16[216,2560]{1,0:T(8,128)(2,1)S(1)}, u32[]{:S(2)}) copy-start(bf16[216,2560]{1,0:T(8,128)(2,1)S(1)} %collective-permute-done.11) | copy-start | bytes 3317764
  76.6 31.7 %collective-permute-start.12 = (bf16[216,2560]{1,0:T(8,128)(2,1)S(1)}, bf16[216,2560]{1,0:T(8,128)(2,1)S(1)}, u32[]{:S(2)}, u32[]{:S(2)}) collective-permute-start(bf16[216,2560]{1,0:T(8,128)(2,1)S(1)} %collective-permute-done.11), channel_id=1, source_target_pairs={{0,30},{2,0},{4,2},{6,4},{8,6},{10,8},{12,10},{14,12},{16,14},{18,... | collective-permute-start | bytes 3317768 | tf_op jit(solution)/shard_map/ppermute | solution.py:89
  81.2 28.1 %collective-permute-start.6 = (bf16[216,2560]{1,0:T(8,128)(2,1)}, bf16[216,2560]{1,0:T(8,128)(2,1)S(1)}, u32[]{:S(2)}, u32[]{:S(2)}) collective-permute-start(bf16[216,2560]{1,0:T(8,128)(2,1)} %collective-permute-done.5), channel_id=1, source_target_pairs={{0,2},{2,4},{4,6},{6,8},{8,10},{10,12},{12,14},{14,16},{16,18},{18... | collective-permute-start | bytes 3317768 | tf_op jit(solution)/shard_map/ppermute | solution.py:87
  106.8 75.2 %collective-permute-start.18 = (bf16[4,4,32,2560]{3,2,1,0:T(8,128)(2,1)}, bf16[4,4,32,2560]{3,2,1,0:T(8,128)(2,1)}, u32[]{:S(2)}, u32[]{:S(2)}) collective-permute-start(bf16[4,4,32,2560]{3,2,1,0:T(8,128)(2,1)} %broadcast_select_fusion.1), channel_id=1, source_target_pairs={{0,1},{1,0},{2,3},{3,2},{4,5},{5,4},{6,7},{7,6},{8,9},{9,8},{10,11... | collective-permute-start | bytes 7864328 | tf_op jit(solution)/shard_map/ppermute | solution.py:16
  108.3 1.0 copy-start.13
  109.4 20.2 %collective-permute-start.13 = (bf16[216,2560]{1,0:T(8,128)(2,1)S(1)}, bf16[216,2560]{1,0:T(8,128)(2,1)S(1)}, u32[]{:S(2)}, u32[]{:S(2)}) collective-permute-start(bf16[216,2560]{1,0:T(8,128)(2,1)S(1)} %collective-permute-done.12), channel_id=1, source_target_pairs={{0,30},{2,0},{4,2},{6,4},{8,6},{10,8},{12,10},{14,12},{16,14},{18,... | collective-permute-start | bytes 3317768 | tf_op jit(solution)/shard_map/ppermute | solution.py:89
  109.4 46.8 %copy-start.17 = (bf16[216,2560]{1,0:T(8,128)(2,1)}, bf16[216,2560]{1,0:T(8,128)(2,1)S(1)}, u32[]{:S(2)}) copy-start(bf16[216,2560]{1,0:T(8,128)(2,1)S(1)} %collective-permute-done.6) | copy-start | bytes 3317764
  109.4 22.6 %collective-permute-start.7 = (bf16[216,2560]{1,0:T(8,128)(2,1)S(1)}, bf16[216,2560]{1,0:T(8,128)(2,1)S(1)}, u32[]{:S(2)}, u32[]{:S(2)}) collective-permute-start(bf16[216,2560]{1,0:T(8,128)(2,1)S(1)} %collective-permute-done.6), channel_id=1, source_target_pairs={{0,2},{2,4},{4,6},{6,8},{8,10},{10,12},{12,14},{14,16},{16,18},{18... | collective-permute-start | bytes 3317768 | tf_op jit(solution)/shard_map/ppermute | solution.py:87
  129.6 1.0 copy-start.15
  130.6 25.6 %collective-permute-start.14 = (bf16[216,2560]{1,0:T(8,128)(2,1)S(1)}, bf16[216,2560]{1,0:T(8,128)(2,1)}, u32[]{:S(2)}, u32[]{:S(2)}) collective-permute-start(bf16[216,2560]{1,0:T(8,128)(2,1)S(1)} %collective-permute-done.13), channel_id=1, source_target_pairs={{0,30},{2,0},{4,2},{6,4},{8,6},{10,8},{12,10},{14,12},{16,14},{18,... | collective-permute-start | bytes 3317768 | tf_op jit(solution)/shard_map/ppermute | solution.py:89
  132.0 24.2 %copy-start.19 = (bf16[216,2560]{1,0:T(8,128)(2,1)}, bf16[216,2560]{1,0:T(8,128)(2,1)S(1)}, u32[]{:S(2)}) copy-start(bf16[216,2560]{1,0:T(8,128)(2,1)S(1)} %collective-permute-done.7) | copy-start | bytes 3317764
  132.0 26.7 %collective-permute-start.8 = (bf16[216,2560]{1,0:T(8,128)(2,1)S(1)}, bf16[216,2560]{1,0:T(8,128)(2,1)}, u32[]{:S(2)}, u32[]{:S(2)}) collective-permute-start(bf16[216,2560]{1,0:T(8,128)(2,1)S(1)} %collective-permute-done.7), channel_id=1, source_target_pairs={{0,2},{2,4},{4,6},{6,8},{8,10},{10,12},{12,14},{14,16},{16,18},{18... | collective-permute-start | bytes 3317768 | tf_op jit(solution)/shard_map/ppermute | solution.py:87
  156.2 29.5 %collective-permute-start.15 = (bf16[216,2560]{1,0:T(8,128)(2,1)}, bf16[216,2560]{1,0:T(8,128)(2,1)}, u32[]{:S(2)}, u32[]{:S(2)}) collective-permute-start(bf16[216,2560]{1,0:T(8,128)(2,1)} %collective-permute-done.14), channel_id=1, source_target_pairs={{0,30},{2,0},{4,2},{6,4},{8,6},{10,8},{12,10},{14,12},{16,14},{18,... | collective-permute-start | bytes 3317768 | tf_op jit(solution)/shard_map/ppermute | solution.py:89
  158.7 27.1 %collective-permute-start.9 = (bf16[216,2560]{1,0:T(8,128)(2,1)}, bf16[216,2560]{1,0:T(8,128)(2,1)}, u32[]{:S(2)}, u32[]{:S(2)}) collective-permute-start(bf16[216,2560]{1,0:T(8,128)(2,1)} %collective-permute-done.8), channel_id=1, source_target_pairs={{0,2},{2,4},{4,6},{6,8},{8,10},{10,12},{12,14},{14,16},{16,18},{18... | collective-permute-start | bytes 3317768 | tf_op jit(solution)/shard_map/ppermute | solution.py:87
  182.0 9.6 %copy-start.20 = (bf16[216,2560]{1,0:T(8,128)(2,1)S(1)}, bf16[216,2560]{1,0:T(8,128)(2,1)}, u32[]{:S(2)}) copy-start(bf16[216,2560]{1,0:T(8,128)(2,1)} %copy-done.19) | copy-start | bytes 3317764
  182.0 10.7 %copy-start.18 = (bf16[216,2560]{1,0:T(8,128)(2,1)S(1)}, bf16[216,2560]{1,0:T(8,128)(2,1)}, u32[]{:S(2)}) copy-start(bf16[216,2560]{1,0:T(8,128)(2,1)} %copy-done.17) | copy-start | bytes 3317764
  185.7 144.1 %copy-start = (bf16[4,4,32,2560]{3,2,1,0:T(8,128)(2,1)}, bf16[4,4,32,2560]{3,2,1,0:T(8,128)(2,1)S(1)}, u32[]{:S(2)}) copy-start(bf16[4,4,32,2560]{3,2,1,0:T(8,128)(2,1)S(1)} %get-tuple-element.32) | copy-start | bytes 7864324
  185.7 10.5 %copy-start.12 = (bf16[216,2560]{1,0:T(8,128)(2,1)S(1)}, bf16[216,2560]{1,0:T(8,128)(2,1)}, u32[]{:S(2)}) copy-start(bf16[216,2560]{1,0:T(8,128)(2,1)} %copy-done.11) | copy-start | bytes 3317764
  185.7 11.6 %copy-start.8 = (bf16[216,2560]{1,0:T(8,128)(2,1)S(1)}, bf16[216,2560]{1,0:T(8,128)(2,1)}, u32[]{:S(2)}) copy-start(bf16[216,2560]{1,0:T(8,128)(2,1)} %copy-done.7) | copy-start | bytes 3317764
  185.7 23.9 %collective-permute-start.16 = (bf16[216,2560]{1,0:T(8,128)(2,1)}, bf16[216,2560]{1,0:T(8,128)(2,1)S(1)}, u32[]{:S(2)}, u32[]{:S(2)}) collective-permute-start(bf16[216,2560]{1,0:T(8,128)(2,1)} %collective-permute-done.15), channel_id=1, source_target_pairs={{0,30},{2,0},{4,2},{6,4},{8,6},{10,8},{12,10},{14,12},{16,14},{18,... | collective-permute-start | bytes 3317768 | tf_op jit(solution)/shard_map/ppermute | solution.py:89
  189.2 9.2 %copy-start.4 = (bf16[216,2560]{1,0:T(8,128)(2,1)S(1)}, bf16[216,2560]{1,0:T(8,128)(2,1)}, u32[]{:S(2)}) copy-start(bf16[216,2560]{1,0:T(8,128)(2,1)} %copy-done.3) | copy-start | bytes 3317764
  191.6 7.9 %copy-start.2 = (bf16[216,2560]{1,0:T(8,128)(2,1)S(1)}, bf16[216,2560]{1,0:T(8,128)(2,1)}, u32[]{:S(2)}) copy-start(bf16[216,2560]{1,0:T(8,128)(2,1)} %param.7) | copy-start | bytes 3317764
  192.7 8.0 %copy-start.6 = (bf16[216,2560]{1,0:T(8,128)(2,1)S(1)}, bf16[216,2560]{1,0:T(8,128)(2,1)}, u32[]{:S(2)}) copy-start(bf16[216,2560]{1,0:T(8,128)(2,1)} %copy-done.5) | copy-start | bytes 3317764
  193.8 8.0 %copy-start.10 = (bf16[216,2560]{1,0:T(8,128)(2,1)S(1)}, bf16[216,2560]{1,0:T(8,128)(2,1)}, u32[]{:S(2)}) copy-start(bf16[216,2560]{1,0:T(8,128)(2,1)} %copy-done.9) | copy-start | bytes 3317764
  196.2 6.7 %copy-start.14 = (bf16[216,2560]{1,0:T(8,128)(2,1)S(1)}, bf16[216,2560]{1,0:T(8,128)(2,1)}, u32[]{:S(2)}) copy-start(bf16[216,2560]{1,0:T(8,128)(2,1)} %copy-done.13) | copy-start | bytes 3317764
  197.3 6.6 %copy-start.16 = (bf16[216,2560]{1,0:T(8,128)(2,1)S(1)}, bf16[216,2560]{1,0:T(8,128)(2,1)}, u32[]{:S(2)}) copy-start(bf16[216,2560]{1,0:T(8,128)(2,1)} %copy-done.15) | copy-start | bytes 3317764
  268.8 42.4 %copy-start.21 = (bf16[1,8,4,32,128]{4,3,2,1,0:T(8,128)(2,1)S(1)}, bf16[1,8,4,32,128]{4,3,2,1,0:T(8,128)(2,1)}, u32[]{:S(2)}) copy-start(bf16[1,8,4,32,128]{4,3,2,1,0:T(8,128)(2,1)} %param.5) | copy-start | bytes 786436
  270.1 24.9 %collective-permute-start.19 = (f32[8,1,32,128]{3,2,1,0:T(8,128)S(1)}, f32[8,1,32,128]{3,2,1,0:T(8,128)S(1)}, u32[]{:S(2)}, u32[]{:S(2)}) collective-permute-start(f32[8,1,32,128]{3,2,1,0:T(8,128)S(1)} %get-tuple-element.35), channel_id=1, source_target_pairs={{0,2},{2,4},{4,6},{1,3},{3,5},{5,7},{8,10},{10,12},{12,14},{9,11},... | collective-permute-start | bytes 393224 | tf_op jit(solution)/shard_map/ppermute | solution.py:41
  293.7 5.2 collective-permute-start.20
  299.0 12.2 %collective-permute-start.21 = (f32[8,4,32,128]{3,2,1,0:T(8,128)S(1)}, f32[8,4,32,128]{3,2,1,0:T(8,128)S(1)}, u32[]{:S(2)}, u32[]{:S(2)}) collective-permute-start(f32[8,4,32,128]{3,2,1,0:T(8,128)S(1)} %slice_add_fusion), channel_id=1, source_target_pairs={{0,1},{1,0},{2,3},{3,2},{4,5},{5,4},{6,7},{7,6},{8,9},{9,8},{10,11... | collective-permute-start | bytes 1572872 | tf_op jit(solution)/shard_map/ppermute | solution.py:16
  300.6 16.1 %copy-start.23 = (f32[8]{0:T(128)}, f32[8]{0:T(128)S(1)}, u32[]{:S(2)}) copy-start(f32[8]{0:T(128)S(1)} %compare_convert_fusion) | copy-start | bytes 100
  312.3 5.9 %collective-permute-start = (bf16[8,1,32,128]{3,2,1,0:T(8,128)(2,1)S(1)}, bf16[8,1,32,128]{3,2,1,0:T(8,128)(2,1)S(1)}, u32[]{:S(2)}, u32[]{:S(2)}) collective-permute-start(bf16[8,1,32,128]{3,2,1,0:T(8,128)(2,1)S(1)} %get-tuple-element.42), channel_id=1, source_target_pairs={{0,2},{2,4},{4,6},{1,3},{3,5},{5,7},{8,10},{10,12},{12,14},{9,11},... | collective-permute-start | bytes 196616 | tf_op jit(solution)/shard_map/ppermute | solution.py:41
  316.7 3.1 collective-permute-start.1
  354.4 0.7 copy-start.22
  354.4 0.7 copy-start.24
  379.3 2.2 copy-start.1
  379.5 58.3 %collective-permute-start.17 = (bf16[4,4,32,2560]{3,2,1,0:T(8,128)(2,1)S(1)}, bf16[4,4,32,2560]{3,2,1,0:T(8,128)(2,1)S(1)}, u32[]{:S(2)}, u32[]{:S(2)}) collective-permute-start(bf16[4,4,32,2560]{3,2,1,0:T(8,128)(2,1)S(1)} %broadcast_select_fusion.3), channel_id=1, source_target_pairs={{0,1},{1,0},{2,3},{3,2},{4,5},{5,4},{6,7},{7,6},{8,9},{9,8},{10,11... | collective-permute-start | bytes 7864328 | tf_op jit(solution)/shard_map/ppermute | solution.py:16
  383.0 3.4 collective-permute-start.22
  386.3 3.7 collective-permute-start.23
  390.0 3.7 collective-permute-start.24
  393.7 6.0 %collective-permute-start.25 = (f32[2560]{0:T(1024)S(1)}, f32[2560]{0:T(1024)S(1)}, u32[]{:S(2)}, u32[]{:S(2)}) collective-permute-start(f32[2560]{0:T(1024)S(1)} %add.221), channel_id=1, source_target_pairs={{0,16},{8,24},{16,0},{24,8},{1,17},{9,25},{17,1},{25,9},{2,18},{10... | collective-permute-start | bytes 30728 | tf_op jit(solution)/shard_map/ppermute | solution.py:16
Sparse Core Ops, SparseCore 0:
  354.6 189.5 reduce-scatter.1
